TPU v7x, 32 devices: a whole 2x2x4 slice. The times are simulated.
32 devices in a mesh: ctx: 8 (over z, y), exp: 4 (over x, core).
Axes of the slice: x: 2, y: 2, z: 4, core: 2. Of those that a mesh axis runs over, the one named last changes fastest.
Arguments:
- scan_grad: bfloat16 [2048, 8192], P('ctx', 'exp'), may hold values from -6 to 6
- step_size: bfloat16 [2048, 8192], P('ctx', 'exp'), may hold values from 0.3 to 4.5, as said below
- scan_input: bfloat16 [2048, 8192], P('ctx', 'exp'), may hold values from -6 to 6
- state_in: float32 [2048, 16], P('ctx'), may hold values from -2 to 2
- state_out: float32 [2048, 16], P('ctx'), may hold values from -0.5 to 0.5
- decay_rate: float32 [16, 8192], P(None, 'exp'), may hold values from -1 to 0, as said below
- skip_gain: float32 [8192], P('exp'), may hold values from 0.5 to 1.5
Outputs:
- scan_input_grad: bfloat16 [2048, 8192], P('ctx', 'exp')
- state_in_grad: float32 [16, 2048], P(None, ('ctx', 'exp'))
Inputs may be any that keep to these rules, and one draw needn't show every extreme that they name: `step_size`: Positive. `decay_rate`: Negative.
All inputs are finite; a program needn't handle non-finite values.
Results may differ from a plain program's by a relative error of at most 0.0015.
Values sent between devices are 32-bit elements; how exact they have to be, the bound alone decides.
A program may use at most 64 MiB of HBM per device.

v0:
```python
import math

import jax
import jax.numpy as jnp
from jax import lax
from jax.sharding import PartitionSpec as P


def carried_in(array, axis, combine, identity):
    size, position = (lax.axis_size(axis), lax.axis_index(axis))
    everything = jax.tree.map(lambda part: lax.all_gather(part, axis), array)
    start = jax.tree.map(
        lambda part, zero: jnp.broadcast_to(jnp.asarray(zero, part.dtype), part.shape),
        array,
        identity,
    )

    def step(k, before):
        at = size - 1 - k
        reached = at > position
        new = combine(before, jax.tree.map(lambda part: part[at], everything))
        return jax.tree.map(lambda a, b: jnp.where(reached, a, b), new, before)

    return lax.fori_loop(0, size, step, start)


def unit_steps(incoming, row_block, decay_rate, skip_gain):
    grad_part, step_part, input_part, in_part, out_part = row_block
    results = []
    b_rows = []
    for offset in range(grad_part.shape[0] - 1, -1, -1):
        grad_row = grad_part[offset].astype(jnp.float32)
        step_row = step_part[offset].astype(jnp.float32)
        input_row = input_part[offset].astype(jnp.float32)
        adjoint = out_part[offset][:, None] * grad_row[None, :] + incoming
        results.append(
            step_row * jnp.sum(in_part[offset][:, None] * adjoint, axis=0) + skip_gain * grad_row
        )
        b_rows.append(jnp.sum(adjoint * (step_row * input_row)[None, :], axis=1))
        incoming = jnp.exp(step_row[None, :] * decay_rate) * adjoint
    return (incoming, (jnp.stack(results[::-1]), jnp.stack(b_rows[::-1])))


def local_sweep(
    scan_grad, step_size, scan_input, state_in, state_out, decay_rate, skip_gain, incoming
):
    row_count, channels = scan_grad.shape
    block_size = 32
    block_count = row_count // block_size

    def sweep_block(carry_state, row_block):
        return unit_steps(carry_state, row_block, decay_rate, skip_gain)

    stacked = (
        scan_grad.reshape(block_count, block_size, channels),
        step_size.reshape(block_count, block_size, channels),
        scan_input.reshape(block_count, block_size, channels),
        state_in.reshape(block_count, block_size, -1),
        state_out.reshape(block_count, block_size, -1),
    )
    final_state, outputs = lax.scan(sweep_block, incoming, stacked, reverse=True)
    grads_all, b_all = outputs
    return (final_state, grads_all.reshape(row_count, channels), b_all.reshape(row_count, -1))


def running_steps(step_size):
    row_count = step_size.shape[0]
    row_index = lax.broadcasted_iota(jnp.int32, (row_count, row_count), 0)
    column_index = lax.broadcasted_iota(jnp.int32, (row_count, row_count), 1)
    tri_table = column_index <= row_index
    return jnp.dot(tri_table.astype(jnp.bfloat16), step_size, preferred_element_type=jnp.float32)


def group_summary(scan_grad, reach_sum, state_out, decay_rate):
    row_count, channels = scan_grad.shape
    block_size = 32
    block_count = row_count // block_size

    def add_block(accum, pieces):
        reach_part, grad_part, out_part = pieces
        decay_weight = jnp.exp(decay_rate[None, :, :] * reach_part[:, None, :])
        term = jnp.einsum(
            "tnc,tn,tc->nc",
            decay_weight,
            out_part,
            grad_part.astype(jnp.float32),
            precision=lax.Precision.HIGHEST,
        )
        return (accum + term, None)

    pieces = (
        reach_sum.reshape(block_count, block_size, channels),
        scan_grad.reshape(block_count, block_size, channels),
        state_out.reshape(block_count, block_size, -1),
    )
    summary, _ = lax.scan(add_block, jnp.zeros(decay_rate.shape, jnp.float32), pieces)
    return summary


def carry_in(total_decay, summary):

    def combine(earlier, later):
        return (later[0] * earlier[0], later[0] * earlier[1] + later[1])

    neutral = (jnp.ones_like(total_decay), jnp.zeros_like(summary))
    return carried_in((total_decay, summary), "ctx", combine, neutral)[1]


def shards(scan_grad, step_size, scan_input, state_in, state_out, decay_rate, skip_gain):
    num_rows = scan_grad.shape[0]
    reach_sum = running_steps(step_size)
    summary = group_summary(scan_grad, reach_sum, state_out, decay_rate)
    total_decay = jnp.exp(decay_rate * reach_sum[num_rows - 1][None, :])
    carried = carry_in(total_decay, summary)
    _, input_grad, b_local = local_sweep(
        scan_grad, step_size, scan_input, state_in, state_out, decay_rate, skip_gain, carried
    )
    scan_input_grad = input_grad.astype(jnp.bfloat16)
    all_channels = scan_grad.shape[1] * lax.axis_size("exp")
    b_term = jnp.transpose(b_local) * (1.0 / math.sqrt(all_channels))
    state_in_grad = lax.psum_scatter(b_term, "exp", scatter_dimension=1, tiled=True)
    return (scan_input_grad, state_in_grad)


def solution(mesh):
    in_specs = (
        P("ctx", "exp"),
        P("ctx", "exp"),
        P("ctx", "exp"),
        P("ctx", None),
        P("ctx", None),
        P(None, "exp"),
        P("exp"),
    )
    out_specs = (P("ctx", "exp"), P(None, ("ctx", "exp")))
    return jax.shard_map(shards, mesh=mesh, in_specs=in_specs, out_specs=out_specs, check_vma=False)
```

profile of v0, /device:TPU:0, one launch (start us, length us, event | category | flops | bytes accessed | tf_op | source)
XLA Modules:
  0.0 338.5 jit_solution(4256488319986549978)
XLA Ops:
  7.2 1.7 fusion.161
  9.0 16.6 %while.46 = (s32[]{:T(128)}, f32[16,2048]{1,0:T(8,128)S(1)}, f32[16,2048]{1,0:T(8,128)S(1)}, f32[8,32,2048]{2,1,0:T(8,128)S(1)}, f32[8,32,16]{1,0,2:T(8,128)S(1)...) while((s32[]{:T(128)}, f32[16,2048]{1,0:T(8,128)S(1)}, f32[16,2048]{1,0:T(8,128)S(1)}, ...), condition=%wide.region_1.2_spmd.clone, body=%wide.region_0.1_spmd.clone.sunk | while | flops 4292611 | bytes 2107499 | solution.py:96
  27.3 42.0 %all-gather.7.cloned.1.call-done = f32[128,2048]{1,0:T(8,128)} async-done(((f32[16,2048]{1,0:T(8,128)}), f32[128,2048]{1,0:T(8,128)}) %all-gather.7.cloned.1.call-update) | async-done | bytes 1048592 | tf_op jit(solution)/shard_map/all_gather | solution.py:11
  69.4 41.7 %all-gather.5.cloned.1.call-done = f32[128,2048]{1,0:T(8,128)} async-done(((f32[16,2048]{1,0:T(8,128)}), f32[128,2048]{1,0:T(8,128)}) %all-gather.5.cloned.1.call-update) | async-done | bytes 1048592 | tf_op jit(solution)/shard_map/all_gather | solution.py:11
  111.1 8.8 %while.47 = (s32[]{:T(128)}, f32[16,2048]{1,0:T(8,128)S(1)}, s32[]{:T(128)}, f32[8,16,2048]{2,1,0:T(8,128)}, f32[8,16,2048]{2,1,0:T(8,128)}, /*index=5*/s32[]{:T(128)}, s32[]{:T(128)}, s32[]{:T(128)}, s32[]{:T(128)}) while((s32[]{:T(128)}, f32[16,2048]{1,0:T(8,128)S(1)}, s32[]{:T(128)}, f32[8,16,2048]{2,1,0:T(8,128)}, ...), condition=%wide.region_3.4_spmd.clone, body=%wide.region_2.3_spmd.clone.sunk | while | flops 131080 | bytes 524451 | solution.py:24
  120.6 189.7 %while.45 = (s32[]{:T(128)}, f32[16,2048]{1,0:T(8,128)S(1)}, bf16[8,32,2048]{2,1,0:T(8,128)(2,1)S(1)}, f32[8,32,16]{2,1,0:T(8,128)}, bf16[8,32,2048]{2,1,0:T(8,1...) while((s32[]{:T(128)}, f32[16,2048]{1,0:T(8,128)S(1)}, ...), condition=%wide.region_69.70_spmd, body=%wide.region_4.69_spmd.sunk | while | flops 10878498 | bytes 10835745 | solution.py:61
  120.6 1.4 fusion.182
  122.1 1.5 fusion.179
  123.6 1.5 fusion.183
  127.4 1.3 fusion.178
  128.7 1.3 fusion.180
  131.2 1.3 fusion.185
  133.9 1.7 multiply_reduce_fusion.76
  144.2 1.5 fusion.182
  145.6 1.5 fusion.179
  147.2 1.5 fusion.183
  152.3 1.4 fusion.180
  154.9 1.3 fusion.185
  157.6 1.7 multiply_reduce_fusion.76
  167.9 1.5 fusion.182
  169.4 1.5 fusion.179
  170.8 1.5 fusion.183
  174.7 1.3 fusion.178
  176.0 1.3 fusion.180
  178.5 1.3 fusion.185
  181.1 1.7 multiply_reduce_fusion.76
  191.4 1.5 fusion.182
  192.9 1.7 fusion.179
  194.7 1.5 fusion.183
  198.5 1.3 fusion.178
  199.8 1.3 fusion.180
  202.3 1.3 fusion.185
  205.0 1.7 multiply_reduce_fusion.76
  215.2 1.5 fusion.182
  216.7 1.5 fusion.179
  218.2 1.7 fusion.183
  222.3 1.5 fusion.178
  223.8 1.3 fusion.180
  226.3 1.3 fusion.185
  229.0 1.7 multiply_reduce_fusion.76
  239.3 1.5 fusion.182
  240.8 1.5 fusion.179
  242.3 1.5 fusion.183
  246.2 1.3 fusion.178
  247.5 1.3 fusion.180
  249.9 1.4 fusion.185
  252.7 1.7 multiply_reduce_fusion.76
  262.9 1.5 fusion.182
  264.4 1.5 fusion.179
  265.9 1.5 fusion.183
  269.8 1.5 fusion.178
  271.3 1.3 fusion.180
  273.8 1.3 fusion.185
  276.5 1.7 multiply_reduce_fusion.76
  286.7 1.5 fusion.182
  288.2 1.5 fusion.179
  289.7 1.5 fusion.183
  293.6 1.3 fusion.178
  294.9 1.4 fusion.180
  297.4 1.3 fusion.185
  300.1 1.7 multiply_reduce_fusion.76
  310.4 1.7 broadcast_multiply_fusion
  312.1 18.5 %reduce-scatter.4.cloned.1.call-done = f32[64,16]{1,0:T(8,128)} async-done(((f32[256,16]{1,0:T(8,128)}), f32[64,16]{1,0:T(8,128)}) %reduce-scatter.4.cloned.1.call-update) | async-done | bytes 4112
  330.6 1.4 copy.30
  (1003 shorter events, 132.6 us)
Async XLA Ops:
  7.2 62.2 %all-gather.7.cloned.1.call-start = ((), (), s32[]{:S(2)}) async-start(), calls=%async_computation.2 | async-start | bytes 1179648 | tf_op jit(solution)/shard_map/all_gather | solution.py:11
  9.0 18.2 %copy-start.19 = (f32[256,16]{0,1:T(8,128)S(1)}, f32[256,16]{0,1:T(8,128)}, u32[]{:S(2)}) copy-start(f32[256,16]{0,1:T(8,128)} %param.16) | copy-start | bytes 49156
  26.4 84.7 %all-gather.5.cloned.1.call-start = ((), (), s32[]{:S(2)}) async-start(), calls=%async_computation.1 | async-start | bytes 1179648 | tf_op jit(solution)/shard_map/all_gather | solution.py:11
  27.1 303.5 %reduce-scatter.4.cloned.1.call-start = ((), (), s32[]{:S(2)}) async-start(), calls=%async_computation.3 | async-start | bytes 163840
  27.2 93.4 %copy-start.1 = (f32[2048]{0:T(1024)S(1)}, f32[2048]{0:T(1024)}, u32[]{:S(2)}) copy-start(f32[2048]{0:T(1024)} %param.19) | copy-start | bytes 24580
  120.6 12.6 %copy-start.4 = (f32[8,32,16]{2,1,0:T(8,128)}, f32[8,32,16]{2,1,0:T(8,128)S(1)}, u32[]{:S(2)}) copy-start(f32[8,32,16]{2,1,0:T(8,128)S(1)} %get-tuple-element.1633) | copy-start | bytes 49156 | tf_op jit(solution)/shard_map/while
  135.5 5.5 %copy-start.12 = (f32[16]{0:T(128)S(1)}, f32[16]{0:T(128)}, u32[]{:S(2)}) copy-start(f32[16]{0:T(128)} %get-tuple-element.1285) | copy-start | bytes 196 | tf_op jit(solution)/shard_map/while
  135.5 5.5 %copy-start.13 = (f32[16]{0:T(128)S(1)}, f32[16]{0:T(128)}, u32[]{:S(2)}) copy-start(f32[16]{0:T(128)} %get-tuple-element.1281) | copy-start | bytes 196 | tf_op jit(solution)/shard_map/while
  135.6 6.0 %copy-start.10 = (f32[16]{0:T(128)S(1)}, f32[16]{0:T(128)}, u32[]{:S(2)}) copy-start(f32[16]{0:T(128)} %get-tuple-element.1272) | copy-start | bytes 196 | tf_op jit(solution)/shard_map/while
  135.6 6.0 %copy-start.11 = (f32[16]{0:T(128)S(1)}, f32[16]{0:T(128)}, u32[]{:S(2)}) copy-start(f32[16]{0:T(128)} %get-tuple-element.1268) | copy-start | bytes 196 | tf_op jit(solution)/shard_map/while
  136.9 5.2 %copy-start.16 = (f32[16]{0:T(128)S(1)}, f32[16]{0:T(128)}, u32[]{:S(2)}) copy-start(f32[16]{0:T(128)} %get-tuple-element.1205) | copy-start | bytes 196 | tf_op jit(solution)/shard_map/while
  136.9 5.2 %copy-start.17 = (f32[16]{0:T(128)S(1)}, f32[16]{0:T(128)}, u32[]{:S(2)}) copy-start(f32[16]{0:T(128)} %get-tuple-element.1206) | copy-start | bytes 196 | tf_op jit(solution)/shard_map/while
  138.2 4.2 %copy-start.7 = (f32[16]{0:T(128)S(1)}, f32[16]{0:T(128)}, u32[]{:S(2)}) copy-start(f32[16]{0:T(128)} %get-tuple-element.1459) | copy-start | bytes 196 | tf_op jit(solution)/shard_map/while
  138.2 4.2 %copy-start.8 = (f32[16]{0:T(128)S(1)}, f32[16]{0:T(128)}, u32[]{:S(2)}) copy-start(f32[16]{0:T(128)} %get-tuple-element.1454) | copy-start | bytes 196 | tf_op jit(solution)/shard_map/while
  144.1 12.8 %copy-start.4 = (f32[8,32,16]{2,1,0:T(8,128)}, f32[8,32,16]{2,1,0:T(8,128)S(1)}, u32[]{:S(2)}) copy-start(f32[8,32,16]{2,1,0:T(8,128)S(1)} %get-tuple-element.1633) | copy-start | bytes 49156 | tf_op jit(solution)/shard_map/while
  159.2 5.5 %copy-start.12 = (f32[16]{0:T(128)S(1)}, f32[16]{0:T(128)}, u32[]{:S(2)}) copy-start(f32[16]{0:T(128)} %get-tuple-element.1285) | copy-start | bytes 196 | tf_op jit(solution)/shard_map/while
  159.2 5.5 %copy-start.13 = (f32[16]{0:T(128)S(1)}, f32[16]{0:T(128)}, u32[]{:S(2)}) copy-start(f32[16]{0:T(128)} %get-tuple-element.1281) | copy-start | bytes 196 | tf_op jit(solution)/shard_map/while
  159.3 6.0 %copy-start.10 = (f32[16]{0:T(128)S(1)}, f32[16]{0:T(128)}, u32[]{:S(2)}) copy-start(f32[16]{0:T(128)} %get-tuple-element.1272) | copy-start | bytes 196 | tf_op jit(solution)/shard_map/while
  159.3 6.0 %copy-start.11 = (f32[16]{0:T(128)S(1)}, f32[16]{0:T(128)}, u32[]{:S(2)}) copy-start(f32[16]{0:T(128)} %get-tuple-element.1268) | copy-start | bytes 196 | tf_op jit(solution)/shard_map/while
  160.6 5.2 %copy-start.16 = (f32[16]{0:T(128)S(1)}, f32[16]{0:T(128)}, u32[]{:S(2)}) copy-start(f32[16]{0:T(128)} %get-tuple-element.1205) | copy-start | bytes 196 | tf_op jit(solution)/shard_map/while
  160.6 5.2 %copy-start.17 = (f32[16]{0:T(128)S(1)}, f32[16]{0:T(128)}, u32[]{:S(2)}) copy-start(f32[16]{0:T(128)} %get-tuple-element.1206) | copy-start | bytes 196 | tf_op jit(solution)/shard_map/while
  167.8 12.6 %copy-start.4 = (f32[8,32,16]{2,1,0:T(8,128)}, f32[8,32,16]{2,1,0:T(8,128)S(1)}, u32[]{:S(2)}) copy-start(f32[8,32,16]{2,1,0:T(8,128)S(1)} %get-tuple-element.1633) | copy-start | bytes 49156 | tf_op jit(solution)/shard_map/while
  182.8 5.5 %copy-start.12 = (f32[16]{0:T(128)S(1)}, f32[16]{0:T(128)}, u32[]{:S(2)}) copy-start(f32[16]{0:T(128)} %get-tuple-element.1285) | copy-start | bytes 196 | tf_op jit(solution)/shard_map/while
  182.8 5.5 %copy-start.13 = (f32[16]{0:T(128)S(1)}, f32[16]{0:T(128)}, u32[]{:S(2)}) copy-start(f32[16]{0:T(128)} %get-tuple-element.1281) | copy-start | bytes 196 | tf_op jit(solution)/shard_map/while
  182.8 6.0 %copy-start.10 = (f32[16]{0:T(128)S(1)}, f32[16]{0:T(128)}, u32[]{:S(2)}) copy-start(f32[16]{0:T(128)} %get-tuple-element.1272) | copy-start | bytes 196 | tf_op jit(solution)/shard_map/while
  182.8 6.0 %copy-start.11 = (f32[16]{0:T(128)S(1)}, f32[16]{0:T(128)}, u32[]{:S(2)}) copy-start(f32[16]{0:T(128)} %get-tuple-element.1268) | copy-start | bytes 196 | tf_op jit(solution)/shard_map/while
  184.1 5.2 %copy-start.16 = (f32[16]{0:T(128)S(1)}, f32[16]{0:T(128)}, u32[]{:S(2)}) copy-start(f32[16]{0:T(128)} %get-tuple-element.1205) | copy-start | bytes 196 | tf_op jit(solution)/shard_map/while
  184.1 5.2 %copy-start.17 = (f32[16]{0:T(128)S(1)}, f32[16]{0:T(128)}, u32[]{:S(2)}) copy-start(f32[16]{0:T(128)} %get-tuple-element.1206) | copy-start | bytes 196 | tf_op jit(solution)/shard_map/while
  191.4 12.9 %copy-start.4 = (f32[8,32,16]{2,1,0:T(8,128)}, f32[8,32,16]{2,1,0:T(8,128)S(1)}, u32[]{:S(2)}) copy-start(f32[8,32,16]{2,1,0:T(8,128)S(1)} %get-tuple-element.1633) | copy-start | bytes 49156 | tf_op jit(solution)/shard_map/while
  206.6 5.5 %copy-start.12 = (f32[16]{0:T(128)S(1)}, f32[16]{0:T(128)}, u32[]{:S(2)}) copy-start(f32[16]{0:T(128)} %get-tuple-element.1285) | copy-start | bytes 196 | tf_op jit(solution)/shard_map/while
  206.6 5.5 %copy-start.13 = (f32[16]{0:T(128)S(1)}, f32[16]{0:T(128)}, u32[]{:S(2)}) copy-start(f32[16]{0:T(128)} %get-tuple-element.1281) | copy-start | bytes 196 | tf_op jit(solution)/shard_map/while
  206.7 6.0 %copy-start.10 = (f32[16]{0:T(128)S(1)}, f32[16]{0:T(128)}, u32[]{:S(2)}) copy-start(f32[16]{0:T(128)} %get-tuple-element.1272) | copy-start | bytes 196 | tf_op jit(solution)/shard_map/while
  206.7 6.0 %copy-start.11 = (f32[16]{0:T(128)S(1)}, f32[16]{0:T(128)}, u32[]{:S(2)}) copy-start(f32[16]{0:T(128)} %get-tuple-element.1268) | copy-start | bytes 196 | tf_op jit(solution)/shard_map/while
  207.9 5.2 %copy-start.16 = (f32[16]{0:T(128)S(1)}, f32[16]{0:T(128)}, u32[]{:S(2)}) copy-start(f32[16]{0:T(128)} %get-tuple-element.1205) | copy-start | bytes 196 | tf_op jit(solution)/shard_map/while
  208.0 5.2 %copy-start.17 = (f32[16]{0:T(128)S(1)}, f32[16]{0:T(128)}, u32[]{:S(2)}) copy-start(f32[16]{0:T(128)} %get-tuple-element.1206) | copy-start | bytes 196 | tf_op jit(solution)/shard_map/while
  215.2 13.1 %copy-start.4 = (f32[8,32,16]{2,1,0:T(8,128)}, f32[8,32,16]{2,1,0:T(8,128)S(1)}, u32[]{:S(2)}) copy-start(f32[8,32,16]{2,1,0:T(8,128)S(1)} %get-tuple-element.1633) | copy-start | bytes 49156 | tf_op jit(solution)/shard_map/while
  230.6 5.5 %copy-start.12 = (f32[16]{0:T(128)S(1)}, f32[16]{0:T(128)}, u32[]{:S(2)}) copy-start(f32[16]{0:T(128)} %get-tuple-element.1285) | copy-start | bytes 196 | tf_op jit(solution)/shard_map/while
  230.6 5.5 %copy-start.13 = (f32[16]{0:T(128)S(1)}, f32[16]{0:T(128)}, u32[]{:S(2)}) copy-start(f32[16]{0:T(128)} %get-tuple-element.1281) | copy-start | bytes 196 | tf_op jit(solution)/shard_map/while
  230.7 6.0 %copy-start.10 = (f32[16]{0:T(128)S(1)}, f32[16]{0:T(128)}, u32[]{:S(2)}) copy-start(f32[16]{0:T(128)} %get-tuple-element.1272) | copy-start | bytes 196 | tf_op jit(solution)/shard_map/while
  230.7 6.0 %copy-start.11 = (f32[16]{0:T(128)S(1)}, f32[16]{0:T(128)}, u32[]{:S(2)}) copy-start(f32[16]{0:T(128)} %get-tuple-element.1268) | copy-start | bytes 196 | tf_op jit(solution)/shard_map/while
  232.0 5.2 %copy-start.16 = (f32[16]{0:T(128)S(1)}, f32[16]{0:T(128)}, u32[]{:S(2)}) copy-start(f32[16]{0:T(128)} %get-tuple-element.1205) | copy-start | bytes 196 | tf_op jit(solution)/shard_map/while
  232.0 5.2 %copy-start.17 = (f32[16]{0:T(128)S(1)}, f32[16]{0:T(128)}, u32[]{:S(2)}) copy-start(f32[16]{0:T(128)} %get-tuple-element.1206) | copy-start | bytes 196 | tf_op jit(solution)/shard_map/while
  239.3 12.8 %copy-start.4 = (f32[8,32,16]{2,1,0:T(8,128)}, f32[8,32,16]{2,1,0:T(8,128)S(1)}, u32[]{:S(2)}) copy-start(f32[8,32,16]{2,1,0:T(8,128)S(1)} %get-tuple-element.1633) | copy-start | bytes 49156 | tf_op jit(solution)/shard_map/while
  254.3 5.5 %copy-start.12 = (f32[16]{0:T(128)S(1)}, f32[16]{0:T(128)}, u32[]{:S(2)}) copy-start(f32[16]{0:T(128)} %get-tuple-element.1285) | copy-start | bytes 196 | tf_op jit(solution)/shard_map/while
  254.3 5.5 %copy-start.13 = (f32[16]{0:T(128)S(1)}, f32[16]{0:T(128)}, u32[]{:S(2)}) copy-start(f32[16]{0:T(128)} %get-tuple-element.1281) | copy-start | bytes 196 | tf_op jit(solution)/shard_map/while
  254.4 6.0 %copy-start.10 = (f32[16]{0:T(128)S(1)}, f32[16]{0:T(128)}, u32[]{:S(2)}) copy-start(f32[16]{0:T(128)} %get-tuple-element.1272) | copy-start | bytes 196 | tf_op jit(solution)/shard_map/while
  254.4 6.0 %copy-start.11 = (f32[16]{0:T(128)S(1)}, f32[16]{0:T(128)}, u32[]{:S(2)}) copy-start(f32[16]{0:T(128)} %get-tuple-element.1268) | copy-start | bytes 196 | tf_op jit(solution)/shard_map/while
  255.7 5.2 %copy-start.16 = (f32[16]{0:T(128)S(1)}, f32[16]{0:T(128)}, u32[]{:S(2)}) copy-start(f32[16]{0:T(128)} %get-tuple-element.1205) | copy-start | bytes 196 | tf_op jit(solution)/shard_map/while
  255.7 5.2 %copy-start.17 = (f32[16]{0:T(128)S(1)}, f32[16]{0:T(128)}, u32[]{:S(2)}) copy-start(f32[16]{0:T(128)} %get-tuple-element.1206) | copy-start | bytes 196 | tf_op jit(solution)/shard_map/while
  262.9 12.9 %copy-start.4 = (f32[8,32,16]{2,1,0:T(8,128)}, f32[8,32,16]{2,1,0:T(8,128)S(1)}, u32[]{:S(2)}) copy-start(f32[8,32,16]{2,1,0:T(8,128)S(1)} %get-tuple-element.1633) | copy-start | bytes 49156 | tf_op jit(solution)/shard_map/while
  278.1 5.5 %copy-start.12 = (f32[16]{0:T(128)S(1)}, f32[16]{0:T(128)}, u32[]{:S(2)}) copy-start(f32[16]{0:T(128)} %get-tuple-element.1285) | copy-start | bytes 196 | tf_op jit(solution)/shard_map/while
  278.1 5.5 %copy-start.13 = (f32[16]{0:T(128)S(1)}, f32[16]{0:T(128)}, u32[]{:S(2)}) copy-start(f32[16]{0:T(128)} %get-tuple-element.1281) | copy-start | bytes 196 | tf_op jit(solution)/shard_map/while
  278.2 6.0 %copy-start.10 = (f32[16]{0:T(128)S(1)}, f32[16]{0:T(128)}, u32[]{:S(2)}) copy-start(f32[16]{0:T(128)} %get-tuple-element.1272) | copy-start | bytes 196 | tf_op jit(solution)/shard_map/while
  278.2 6.0 %copy-start.11 = (f32[16]{0:T(128)S(1)}, f32[16]{0:T(128)}, u32[]{:S(2)}) copy-start(f32[16]{0:T(128)} %get-tuple-element.1268) | copy-start | bytes 196 | tf_op jit(solution)/shard_map/while
  279.4 5.2 %copy-start.16 = (f32[16]{0:T(128)S(1)}, f32[16]{0:T(128)}, u32[]{:S(2)}) copy-start(f32[16]{0:T(128)} %get-tuple-element.1205) | copy-start | bytes 196 | tf_op jit(solution)/shard_map/while
  279.5 5.2 %copy-start.17 = (f32[16]{0:T(128)S(1)}, f32[16]{0:T(128)}, u32[]{:S(2)}) copy-start(f32[16]{0:T(128)} %get-tuple-element.1206) | copy-start | bytes 196 | tf_op jit(solution)/shard_map/while
  286.7 12.7 %copy-start.4 = (f32[8,32,16]{2,1,0:T(8,128)}, f32[8,32,16]{2,1,0:T(8,128)S(1)}, u32[]{:S(2)}) copy-start(f32[8,32,16]{2,1,0:T(8,128)S(1)} %get-tuple-element.1633) | copy-start | bytes 49156 | tf_op jit(solution)/shard_map/while
  301.8 5.5 %copy-start.12 = (f32[16]{0:T(128)S(1)}, f32[16]{0:T(128)}, u32[]{:S(2)}) copy-start(f32[16]{0:T(128)} %get-tuple-element.1285) | copy-start | bytes 196 | tf_op jit(solution)/shard_map/while
  301.8 5.5 %copy-start.13 = (f32[16]{0:T(128)S(1)}, f32[16]{0:T(128)}, u32[]{:S(2)}) copy-start(f32[16]{0:T(128)} %get-tuple-element.1281) | copy-start | bytes 196 | tf_op jit(solution)/shard_map/while
  301.8 6.0 %copy-start.10 = (f32[16]{0:T(128)S(1)}, f32[16]{0:T(128)}, u32[]{:S(2)}) copy-start(f32[16]{0:T(128)} %get-tuple-element.1272) | copy-start | bytes 196 | tf_op jit(solution)/shard_map/while
  301.8 6.0 %copy-start.11 = (f32[16]{0:T(128)S(1)}, f32[16]{0:T(128)}, u32[]{:S(2)}) copy-start(f32[16]{0:T(128)} %get-tuple-element.1268) | copy-start | bytes 196 | tf_op jit(solution)/shard_map/while
  303.1 5.2 %copy-start.16 = (f32[16]{0:T(128)S(1)}, f32[16]{0:T(128)}, u32[]{:S(2)}) copy-start(f32[16]{0:T(128)} %get-tuple-element.1205) | copy-start | bytes 196 | tf_op jit(solution)/shard_map/while
  303.1 5.2 %copy-start.17 = (f32[16]{0:T(128)S(1)}, f32[16]{0:T(128)}, u32[]{:S(2)}) copy-start(f32[16]{0:T(128)} %get-tuple-element.1206) | copy-start | bytes 196 | tf_op jit(solution)/shard_map/while
  310.4 21.6 %copy-start.3 = (bf16[8,32,2048]{2,1,0:T(8,128)(2,1)}, bf16[8,32,2048]{2,1,0:T(8,128)(2,1)S(1)}, u32[]{:S(2)}) copy-start(bf16[8,32,2048]{2,1,0:T(8,128)(2,1)S(1)} %get-tuple-element.386) | copy-start | bytes 3145732
  (57 other events, 220.0 us)
Sparse Core Ops, SparseCore 0:
  26.5 42.8 all-gather.6
  72.1 38.9 all-gather.4
  312.2 18.3 reduce-scatter.3
where the time goes:
time: 345 us; the launch traced here: 339 us
  other arithmetic  161 us (47%)
  waiting for transfers between devices  102 us (30%)
  local copies, waits for them, and re-layouts  54.5 us (16%)
  between operations  13.9 us (4%)
  loops' own time  4.71 us (1%)
    all_gather x2, waiting for transfers between devices, carried_in(): everything = jax.tree.map(lambda part: lax.all_gather(part, axis), array)  83.8 us
    reduce_sum x72, other arithmetic, unit_steps(): b_rows.append(jnp.sum(adjoint * (step_row * input_row)[None, :], axis=1))  61.8 us
    while x480, local copies, waits for them, and re-layouts  24.8 us
    convert_element_type x16, other arithmetic, unit_steps(): grad_row = grad_part[offset].astype(jnp.float32)  22.8 us
    convert_element_type x16, other arithmetic, unit_steps(): input_row = input_part[offset].astype(jnp.float32)  22.7 us
    convert_element_type x16, other arithmetic, unit_steps(): step_row = step_part[offset].astype(jnp.float32)  22.6 us
    unnamed x4, waiting for transfers between devices  18.5 us
    mul x16, local copies, waits for them, and re-layouts, unit_steps(): in_part[offset][:, None] * adjoint  10.5 us
  transfers between devices with their start and end apart: 3, of which 3 were waited for; matrix products, arithmetic and copies ran while one was open for 0% of the time, Pallas kernels for 0%

commit v1 on v0

v1 whole, which is shorter than its diff:
```python
import functools
import math

import jax
import jax.numpy as jnp
from jax import lax
from jax.experimental import pallas as pl
from jax.experimental.pallas import tpu as pltpu
from jax.sharding import PartitionSpec as P

MESH = pl.DeviceIdType.MESH
LANES = 128
TILES = 4
BLOCK = 16
LOG2E = math.log2(math.e)


def kernel(
    n_ctx, n_exp, scale,
    grad_hbm, step_hbm, input_hbm, in_ref, out_ref, rate_ref, gain_ref,
    dx_hbm, db_ref,
    grad_bf, step_bf, input_bf, dx_bf,
    grad_f, step_f, x_f, in_rep, out_rep, partial, transposer, rate2,
    summary, got_a, window, got_b, incoming_e, keep, give, got_c,
    share, got_share,
    load_sem, store_sem, a_sem, b_sem, c_sem, r_sem,
):
    rows, channels = grad_bf.shape[0], grad_hbm.shape[1]
    states = rate_ref.shape[0]
    width = TILES * LANES
    half = width // 2
    groups = channels // width
    blocks = rows // BLOCK
    section = rows // n_exp
    pairs = n_ctx // 2
    hops = []
    while (1 << len(hops)) < pairs:
        hops.append(1 << len(hops))

    ctx, me = lax.axis_index("ctx"), lax.axis_index("exp")
    side = lax.rem(ctx, 2)
    pair = ctx // 2
    partner = ctx + 1 - 2 * side
    low = side == 0

    def load(which, g):
        hbm, vmem = ((step_hbm, step_bf), (grad_hbm, grad_bf), (input_hbm, input_bf))[which]
        cols = pl.ds(g * width, width)
        return pltpu.make_async_copy(hbm.at[:, cols], vmem.at[:, cols], load_sem.at[which, g])

    for g in range(groups):
        load(0, g).start()
        load(1, g).start()
    for g in range(groups):
        load(2, g).start()

    barrier = pltpu.get_barrier_semaphore()
    count = 1 + (n_exp - 1)
    pl.semaphore_signal(barrier, inc=1, device_id=(partner, me), device_id_type=MESH)
    for other in range(1, n_exp):
        pl.semaphore_signal(
            barrier, inc=1, device_id=(ctx, lax.rem(me + other, n_exp)), device_id_type=MESH
        )
    for hop in hops:

        @pl.when(pair + hop < pairs)
        def _():
            pl.semaphore_signal(barrier, inc=1, device_id=(ctx + 2 * hop, me), device_id_type=MESH)

        @pl.when(pair >= hop)
        def _():
            pl.semaphore_signal(barrier, inc=1, device_id=(ctx - 2 * hop, me), device_id_type=MESH)

        count = count + jnp.where(pair + hop < pairs, 1, 0) + jnp.where(pair >= hop, 1, 0)

    for source, target in ((out_ref, out_rep), (in_ref, in_rep)):
        for start in range(0, rows, LANES):
            turned = jnp.transpose(source[start : start + LANES, :])
            for lane in range(LANES):
                target[start + lane] = jnp.broadcast_to(
                    turned[:, lane : lane + 1], (states, LANES)
                )
    for g in range(groups):
        for h in range(2):
            at = g * width + h * half
            rate2[g, h] = rate_ref[:, at : at + half] * LOG2E

    def rates(g):
        per_half = TILES // 2
        return [
            rate2[g, w // per_half, :, (w % per_half) * LANES : (w % per_half + 1) * LANES]
            for w in range(TILES)
        ]

    def columns(g, w):
        return pl.ds(g * width + w * LANES, LANES)

    def first_sweep(g):
        load(0, g).wait()
        load(1, g).wait()
        cols = pl.ds(g * width, width)

        def widen(b, total):
            at = pl.ds(pl.multiple_of(b * BLOCK, BLOCK), BLOCK)
            step = step_bf[at, cols].astype(jnp.float32)
            grad = grad_bf[at, cols].astype(jnp.float32)
            for k in range(BLOCK // 8):
                step_f[b * (BLOCK // 8) + k, :, cols] = step[8 * k : 8 * k + 8]
                grad_f[b * (BLOCK // 8) + k, :, cols] = grad[8 * k : 8 * k + 8]
                total = total + step[8 * k : 8 * k + 8]
            return total

        total = lax.fori_loop(0, blocks, widen, jnp.zeros((8, width), jnp.float32))
        rate = rates(g)

        def sweep(k, carry):
            carry = list(carry)
            b = blocks - 1 - k
            for i in range(BLOCK - 1, -1, -1):
                tile, sub = b * (BLOCK // 8) + i // 8, i % 8
                out = out_rep[b * BLOCK + i]
                for w in range(TILES):
                    step = step_f[tile, sub : sub + 1, columns(g, w)]
                    grad = grad_f[tile, sub : sub + 1, columns(g, w)]
                    carry[w] = jnp.exp2(step * rate[w]) * (out * grad + carry[w])
            return tuple(carry)

        zero = jnp.zeros((states, LANES), jnp.float32)
        carry = lax.fori_loop(0, blocks, sweep, (zero,) * TILES)
        reach = jnp.broadcast_to(jnp.sum(total, axis=0, keepdims=True), (8, width))
        per_half = TILES // 2
        for w in range(TILES):
            lanes = slice((w % per_half) * LANES, (w % per_half + 1) * LANES)
            summary[g, w // per_half, :states, lanes] = carry[w]
        for h in range(2):
            summary[g, h, states:, :] = reach[:, h * half : (h + 1) * half]

    def copy_a(g):
        return pltpu.make_async_remote_copy(
            src_ref=summary.at[g, 1 - side], dst_ref=got_a.at[g],
            send_sem=a_sem.at[0, g], recv_sem=a_sem.at[1, g],
            device_id=(partner, me), device_id_type=MESH,
        )

    def copy_b(g, k):
        return pltpu.make_async_remote_copy(
            src_ref=window.at[g, k], dst_ref=got_b.at[g, k],
            send_sem=b_sem.at[0, g, k], recv_sem=b_sem.at[1, g, k],
            device_id=(ctx - 2 * hops[k], me), device_id_type=MESH,
        )

    def copy_c(g):
        return pltpu.make_async_remote_copy(
            src_ref=give.at[g], dst_ref=got_c.at[g],
            send_sem=c_sem.at[0, g], recv_sem=c_sem.at[1, g],
            device_id=(partner, me), device_id_type=MESH,
        )

    def both_sides(g):
        own, other = summary[g, side], got_a[g]
        return jnp.where(low, own, other), jnp.where(low, other, own)

    def decay(rate, reach):
        return jnp.exp2(rate * jnp.concatenate([reach] * (states // 8), axis=0))

    def send_b(g, k):
        @pl.when(pair >= hops[k])
        def _():
            copy_b(g, k).start()

    def finish(g):
        first, second = both_sides(g)
        entering = incoming_e[g, :states]
        low_value = second[:states] + decay(rate2[g, side], second[states:]) * entering
        keep[g] = jnp.where(low, low_value, entering)
        give[g] = jnp.where(low, entering, low_value)
        copy_c(g).start()

    def stage(g, s):
        if s == 0:
            copy_a(g).start()
            return
        if s == 1:
            copy_a(g).wait_recv()
            first, second = both_sides(g)
            rate = rate2[g, side]
            window[g, 0, :states] = first[:states] + decay(rate, first[states:]) * second[:states]
            window[g, 0, states:] = first[states:] + second[states:]
            incoming_e[g] = jnp.zeros((states + 8, half), jnp.float32)
            if hops:
                send_b(g, 0)
            else:
                finish(g)
            return
        k = s - 2
        rate = rate2[g, side]

        @pl.when(pair + hops[k] < pairs)
        def _():
            copy_b(g, k).wait_recv()
            entering, got = incoming_e[g], got_b[g, k]
            incoming_e[g, :states] = (
                entering[:states] + decay(rate, entering[states:]) * got[:states]
            )
            incoming_e[g, states:] = entering[states:] + got[states:]

        if k + 1 < len(hops):
            mine, entering = window[g, 0], incoming_e[g]
            window[g, k + 1, :states] = (
                mine[:states] + decay(rate, mine[states:]) * entering[:states]
            )
            window[g, k + 1, states:] = mine[states:] + entering[states:]
            send_b(g, k + 1)
        else:
            finish(g)

    stages = 2 + len(hops)
    done = [0] * groups

    def advance(g, limit):
        while done[g] < min(limit, stages):
            stage(g, done[g])
            done[g] += 1

    lane_index = lax.broadcasted_iota(jnp.int32, (states, LANES), 1)

    def second_sweep(g):
        load(2, g).wait()
        cols = pl.ds(g * width, width)

        def widen(b, _):
            at = pl.ds(pl.multiple_of(b * BLOCK, BLOCK), BLOCK)
            part = input_bf[at, cols].astype(jnp.float32)
            for k in range(BLOCK // 8):
                tile = b * (BLOCK // 8) + k
                x_f[tile, :, cols] = part[8 * k : 8 * k + 8] * step_f[tile, :, cols]
            return 0

        lax.fori_loop(0, blocks, widen, 0)
        rate = rates(g)
        copy_c(g).wait_recv()
        mine, other = keep[g], got_c[g]
        halves = (jnp.where(low, mine, other), jnp.where(low, other, mine))
        per_half = TILES // 2
        carry = tuple(
            halves[w // per_half][:, (w % per_half) * LANES : (w % per_half + 1) * LANES]
            for w in range(TILES)
        )
        last = g == groups - 1
        gain = [gain_ref[:, columns(g, w)] for w in range(TILES)]

        def sweep(q, k, state):
            carry, sums = list(state[0]), state[1]
            per_section = section // BLOCK
            b = (q + 1) * per_section - 1 - k
            for i in range(BLOCK - 1, -1, -1):
                tile, sub = b * (BLOCK // 8) + i // 8, i % 8
                at = b * BLOCK + i
                out, inn = out_rep[at], in_rep[at]
                products = None
                for w in range(TILES):
                    step = step_f[tile, sub : sub + 1, columns(g, w)]
                    grad = grad_f[tile, sub : sub + 1, columns(g, w)]
                    x = x_f[tile, sub : sub + 1, columns(g, w)]
                    adjoint = out * grad + carry[w]
                    weighted = inn * adjoint
                    folded = weighted[:8]
                    for s in range(8, states, 8):
                        folded = folded + weighted[s : s + 8]
                    transposer[w, 8 * i : 8 * i + 8, :] = folded
                    product = adjoint * x
                    products = product if products is None else products + product
                    carry[w] = jnp.exp2(step * rate[w]) * adjoint
                if g > 0:
                    products = products + partial[at]
                if last:
                    summed = jnp.sum(products, axis=1, keepdims=True)
                    sums = jnp.where(lane_index == k_lane(b, i, q), summed, sums)
                else:
                    partial[at] = products
            for w in range(TILES):
                results = []
                for h in range(BLOCK // 8):
                    tile = b * (BLOCK // 8) + h
                    total = transposer[w, pl.ds(64 * h, 8, stride=8), :]
                    for s in range(1, 8):
                        total = total + transposer[w, pl.ds(64 * h + s, 8, stride=8), :]
                    results.append(
                        step_f[tile, :, columns(g, w)] * total
                        + gain[w] * grad_f[tile, :, columns(g, w)]
                    )
                dx_bf[pl.ds(pl.multiple_of(b * BLOCK, BLOCK), BLOCK), columns(g, w)] = (
                    jnp.concatenate(results, axis=0).astype(jnp.bfloat16)
                )
            return tuple(carry), sums

        def k_lane(b, i, q):
            return b * BLOCK + i - q * section

        zero = jnp.zeros((states, LANES), jnp.float32)
        if last:
            for q in range(n_exp - 1, -1, -1):
                carry, sums = lax.fori_loop(
                    0, section // BLOCK, functools.partial(sweep, q), (carry, zero)
                )
                share[q] = sums * scale

                @pl.when(me != q)
                def _():
                    copy_share(q).start()
        else:

            def all_rows(k, state):
                carry, _ = sweep_any(k, state)
                return carry, state[1]

            def sweep_any(k, state):
                b = blocks - 1 - k
                per_section = section // BLOCK
                return sweep(n_exp - 1, (n_exp * per_section - 1) - b, state)

            carry, _ = lax.fori_loop(0, blocks, all_rows, (carry, jnp.zeros((8, LANES), jnp.float32)))
        store(g).start()

    def store(g):
        cols = pl.ds(g * width, width)
        return pltpu.make_async_copy(dx_bf.at[:, cols], dx_hbm.at[:, cols], store_sem.at[g])

    def copy_share(q):
        return pltpu.make_async_remote_copy(
            src_ref=share.at[q], dst_ref=got_share.at[me],
            send_sem=r_sem.at[0, q], recv_sem=r_sem.at[1, me],
            device_id=(ctx, q), device_id_type=MESH,
        )

    for g in range(groups):
        first_sweep(g)
        if g == 0:
            pl.semaphore_wait(barrier, count)
        advance(g, 1)
        for earlier in range(g - 1, -1, -1):
            advance(earlier, g - earlier + 1)
    for g in range(groups):
        for later in range(groups - 1, g, -1):
            advance(later, groups + g - later + 1)
        advance(g, stages)
        second_sweep(g)

    total = share[me]
    for q in range(n_exp):

        @pl.when(me != q)
        def _():
            pltpu.make_async_remote_copy(
                src_ref=share.at[q], dst_ref=got_share.at[q],
                send_sem=r_sem.at[0, q], recv_sem=r_sem.at[1, q],
                device_id=(ctx, q), device_id_type=MESH,
            ).wait_recv()

    for other in range(1, n_exp):
        total = total + got_share[lax.rem(me + other, n_exp)]
    db_ref[...] = total[:, :section]

    for q in range(n_exp):

        @pl.when(me != q)
        def _():
            copy_share(q).wait_send()

    for g in range(groups):
        store(g).wait()
        copy_a(g).wait_send()
        copy_c(g).wait_send()
        for k, hop in enumerate(hops):

            @pl.when(pair >= hop)
            def _():
                copy_b(g, k).wait_send()


def shards(scan_grad, step_size, scan_input, state_in, state_out, decay_rate, skip_gain):
    n_ctx, n_exp = lax.axis_size("ctx"), lax.axis_size("exp")
    rows, channels = scan_grad.shape
    states = state_in.shape[1]
    width = TILES * LANES
    groups, half = channels // width, width // 2
    hops = max(1, (n_ctx // 2 - 1).bit_length())
    f32, bf16 = jnp.float32, jnp.bfloat16
    any_spec = pl.BlockSpec(memory_space=pl.ANY)
    vmem = pl.BlockSpec(memory_space=pltpu.VMEM)
    work = rows * channels * states
    return pl.pallas_call(
        functools.partial(kernel, n_ctx, n_exp, 1.0 / math.sqrt(channels * n_exp)),
        out_shape=(
            jax.ShapeDtypeStruct((rows, channels), bf16),
            jax.ShapeDtypeStruct((states, rows // n_exp), f32),
        ),
        in_specs=[any_spec, any_spec, any_spec, vmem, vmem, vmem, vmem],
        out_specs=(any_spec, vmem),
        scratch_shapes=[
            pltpu.VMEM((rows, channels), bf16),
            pltpu.VMEM((rows, channels), bf16),
            pltpu.VMEM((rows, channels), bf16),
            pltpu.VMEM((rows, channels), bf16),
            pltpu.VMEM((rows // 8, 8, channels), f32),
            pltpu.VMEM((rows // 8, 8, channels), f32),
            pltpu.VMEM((rows // 8, 8, channels), f32),
            pltpu.VMEM((rows, states, LANES), f32),
            pltpu.VMEM((rows, states, LANES), f32),
            pltpu.VMEM((rows, states, LANES), f32),
            pltpu.VMEM((TILES, 8 * BLOCK, LANES), f32),
            pltpu.VMEM((groups, 2, states, half), f32),
            pltpu.VMEM((groups, 2, states + 8, half), f32),
            pltpu.VMEM((groups, states + 8, half), f32),
            pltpu.VMEM((groups, hops, states + 8, half), f32),
            pltpu.VMEM((groups, hops, states + 8, half), f32),
            pltpu.VMEM((groups, states + 8, half), f32),
            pltpu.VMEM((groups, states, half), f32),
            pltpu.VMEM((groups, states, half), f32),
            pltpu.VMEM((groups, states, half), f32),
            pltpu.VMEM((n_exp, states, LANES), f32),
            pltpu.VMEM((n_exp, states, LANES), f32),
            pltpu.SemaphoreType.DMA((3, groups)),
            pltpu.SemaphoreType.DMA((groups,)),
            pltpu.SemaphoreType.DMA((2, groups)),
            pltpu.SemaphoreType.DMA((2, groups, hops)),
            pltpu.SemaphoreType.DMA((2, groups)),
            pltpu.SemaphoreType.DMA((2, n_exp)),
        ],
        compiler_params=pltpu.CompilerParams(
            collective_id=0, has_side_effects=True, vmem_limit_bytes=48 * 1024 * 1024
        ),
        cost_estimate=pl.CostEstimate(
            flops=14 * work, bytes_accessed=8 * rows * channels, transcendentals=2 * work
        ),
    )(
        scan_grad, step_size, scan_input, state_in, state_out, decay_rate,
        skip_gain.reshape(1, channels),
    )


def solution(mesh):
    in_specs = (
        P("ctx", "exp"),
        P("ctx", "exp"),
        P("ctx", "exp"),
        P("ctx", None),
        P("ctx", None),
        P(None, "exp"),
        P("exp"),
    )
    out_specs = (P("ctx", "exp"), P(None, ("ctx", "exp")))
    return jax.shard_map(shards, mesh=mesh, in_specs=in_specs, out_specs=out_specs, check_vma=False)
```

time: 345 us -> 44 us (0.13); the launches traced: 339 us -> 43.7 us
  other arithmetic: 161 us -> 0 us
  waiting for transfers between devices: 102 us -> 0 us
  local copies, waits for them, and re-layouts: 54.5 us -> 6.8 us
  Pallas kernels: 0 us -> 36.2 us
  between operations: 13.9 us -> 0.67 us
  loops' own time: 4.71 us -> 0 us
    all_gather x2 -> x0, waiting for transfers between devices: 83.8 us -> none  [carried_in(): everything = jax.tree.map(lambda part: lax.all_gather(part, axis), array)]
    convert_element_type x48 -> x0, other arithmetic: 68.2 us -> none  [the longest x16 22.8 us: unit_steps(): grad_row = grad_part[offset].astype(jnp.float32)]
    reduce_sum x72 -> x0, other arithmetic: 61.8 us -> none  [unit_steps(): b_rows.append(jnp.sum(adjoint * (step_row * input_row)[None, :], axis=1))]
    pallas_call x0 -> x1, Pallas kernels: none -> 36.2 us  [shards(): pl.pallas_call(functools.partial(kernel, n_ctx, n_exp, 1.0 / math.sqrt(ch...]
    while x480 -> x0, local copies, waits for them, and re-layouts: 24.8 us -> none
    unnamed x4 -> x0, waiting for transfers between devices: 18.5 us -> none
    mul x24 -> x0, local copies, waits for them, and re-layouts: 10.7 us -> none  [the longest x16 10.5 us: unit_steps(): in_part[offset][:, None] * adjoint]
    select_n x8 -> x0, other arithmetic: 8.57 us -> none  [step(): return jax.tree.map(lambda a, b: jnp.where(reached, a, b), new, before)]
  transfers between devices with their start and end apart: 3 -> 0, of which waited for: 3 -> 0; matrix products, arithmetic and copies ran while one was open for 0% -> 0% of each run, Pallas kernels for 0% -> 0%
where the time goes in v1:
time: 44 us; the launch traced here: 43.7 us
  Pallas kernels  36.2 us (82%)
  local copies, waits for them, and re-layouts  6.8 us (15%)
  between operations  0.67 us (2%)
    pallas_call x1, Pallas kernels, shards(): pl.pallas_call(functools.partial(kernel, n_ctx, n_exp, 1.0 / math.sqrt(ch...  36.2 us
    unnamed x16, local copies, waits for them, and re-layouts  6.8 us

profile of v1, /device:TPU:0, one launch (start us, length us, event | category | flops | bytes accessed | tf_op | source)
XLA Modules:
  0.0 43.7 jit_solution(6394064750001154129)
XLA Ops:
  0.6 0.0 copy-start.5
  0.6 0.0 copy-start.3
  0.7 0.9 %copy.9.in_ref = f32[256,16]{1,0:T(8,128)S(1)} copy(f32[256,16]{0,1:T(8,128)} %param.10) | data formatting | bytes 32768 | tf_op args[3]
  1.5 0.0 copy-done.5
  1.5 0.0 copy-start.4
  1.5 0.1 copy.10.out_ref
  1.6 0.0 copy-done.3
  1.6 0.6 %copy-done.4 = f32[2048]{0:T(1024)S(1)} copy-done((f32[2048]{0:T(1024)S(1)}, f32[2048]{0:T(1024)}, u32[]{:S(2)}) %copy-start.4) | copy-done | bytes 8216
  2.2 0.0 copy-start
  2.2 1.2 %copy-done = bf16[256,2048]{1,0:T(8,128)(2,1)S(1)} copy-done((bf16[256,2048]{1,0:T(8,128)(2,1)S(1)}, bf16[256,2048]{1,0:T(8,128)(2,1)}, u32[]{:S(2)}) %copy-start) | copy-done | bytes 1048600
  3.4 0.0 copy-start.1
  3.5 1.2 %copy-done.1 = bf16[256,2048]{1,0:T(8,128)(2,1)S(1)} copy-done((bf16[256,2048]{1,0:T(8,128)(2,1)S(1)}, bf16[256,2048]{1,0:T(8,128)(2,1)}, u32[]{:S(2)}) %copy-start.1) | copy-done | bytes 1048600
  4.7 0.0 copy-start.2
  4.7 1.2 %copy-done.2 = bf16[256,2048]{1,0:T(8,128)(2,1)S(1)} copy-done((bf16[256,2048]{1,0:T(8,128)(2,1)S(1)}, bf16[256,2048]{1,0:T(8,128)(2,1)}, u32[]{:S(2)}) %copy-start.2) | copy-done | bytes 1048600
  5.9 36.2 %shard_map.86 = (bf16[256,2048]{1,0:T(8,128)(2,1)S(1)}, f32[16,64]{1,0:T(8,128)S(1)}) custom-call(bf16[256,2048]{1,0:T(8,128)(2,1)S(1)} %copy-done, bf16[256,2048]{1,0:T(8,128)(2,1)S(1)} %copy-done.1, bf16[256,2048]{1,0:T(8,128)(2,1)S(1)} %copy-done.2, f32[256,16]{1,0:T(8,128)S(1)} %copy.9.in_ref, f32[256,16]{1,0:T(8,128)S(1)} %copy.10.out_ref, ...), custom_call_target="tpu_custom_call" | custom-call | flops 117440512 | bytes 4194304 | tf_op jit(solution)/shard_map/pallas_call | solution.py:392
  42.1 1.0 %copy.13 = bf16[256,2048]{1,0:T(8,128)(2,1)} copy(bf16[256,2048]{1,0:T(8,128)(2,1)S(1)} %get-tuple-element.4) | data formatting | bytes 2097152
  43.1 0.6 %copy.14 = f32[16,64]{1,0:T(8,128)} copy(f32[16,64]{1,0:T(8,128)S(1)} %get-tuple-element.5) | data formatting | bytes 8192
Async XLA Ops:
  0.6 0.9 %copy-start.5 = (f32[256,16]{0,1:T(8,128)S(1)}, f32[256,16]{0,1:T(8,128)}, u32[]{:S(2)}) copy-start(f32[256,16]{0,1:T(8,128)} %param.11) | copy-start | bytes 49156
  0.6 1.0 %copy-start.3 = (f32[16,2048]{1,0:T(8,128)S(1)}, f32[16,2048]{1,0:T(8,128)}, u32[]{:S(2)}) copy-start(f32[16,2048]{1,0:T(8,128)} %rate_ref.1) | copy-start | bytes 393220
  1.5 0.7 %copy-start.4 = (f32[2048]{0:T(1024)S(1)}, f32[2048]{0:T(1024)}, u32[]{:S(2)}) copy-start(f32[2048]{0:T(1024)} %param.13) | copy-start | bytes 24580
  2.2 1.2 %copy-start = (bf16[256,2048]{1,0:T(8,128)(2,1)S(1)}, bf16[256,2048]{1,0:T(8,128)(2,1)}, u32[]{:S(2)}) copy-start(bf16[256,2048]{1,0:T(8,128)(2,1)} %grad_hbm.1) | copy-start | bytes 3145732
  3.4 1.2 %copy-start.1 = (bf16[256,2048]{1,0:T(8,128)(2,1)S(1)}, bf16[256,2048]{1,0:T(8,128)(2,1)}, u32[]{:S(2)}) copy-start(bf16[256,2048]{1,0:T(8,128)(2,1)} %step_hbm.1) | copy-start | bytes 3145732
  4.7 1.2 %copy-start.2 = (bf16[256,2048]{1,0:T(8,128)(2,1)S(1)}, bf16[256,2048]{1,0:T(8,128)(2,1)}, u32[]{:S(2)}) copy-start(bf16[256,2048]{1,0:T(8,128)(2,1)} %input_hbm.1) | copy-start | bytes 3145732

commit v2 on v1

--- a/solution.py
+++ b/solution.py
@@ -73,13 +73,15 @@
 
         count = count + jnp.where(pair + hop < pairs, 1, 0) + jnp.where(pair >= hop, 1, 0)
 
-    for source, target in ((out_ref, out_rep), (in_ref, in_rep)):
+    def repeat(source, target):
         for start in range(0, rows, LANES):
-            turned = jnp.transpose(source[start : start + LANES, :])
+            turned = source[:, start : start + LANES]
             for lane in range(LANES):
                 target[start + lane] = jnp.broadcast_to(
                     turned[:, lane : lane + 1], (states, LANES)
                 )
+
+    repeat(out_ref, out_rep)
     for g in range(groups):
         for h in range(2):
             at = g * width + h * half
@@ -92,6 +94,10 @@
             for w in range(TILES)
         ]
 
+    def row(ref, at, tile, sub):
+        once = ref[at, tile, pl.ds(sub, 8, stride=0), :]
+        return jnp.concatenate([once] * (states // 8), axis=0)
+
     def columns(g, w):
         return pl.ds(g * width + w * LANES, LANES)
 
@@ -101,12 +107,14 @@
         cols = pl.ds(g * width, width)
 
         def widen(b, total):
-            at = pl.ds(pl.multiple_of(b * BLOCK, BLOCK), BLOCK)
-            step = step_bf[at, cols].astype(jnp.float32)
-            grad = grad_bf[at, cols].astype(jnp.float32)
+            block = pl.ds(pl.multiple_of(b * BLOCK, BLOCK), BLOCK)
+            step = step_bf[block, cols].astype(jnp.float32)
+            grad = grad_bf[block, cols].astype(jnp.float32)
             for k in range(BLOCK // 8):
-                step_f[b * (BLOCK // 8) + k, :, cols] = step[8 * k : 8 * k + 8]
-                grad_f[b * (BLOCK // 8) + k, :, cols] = grad[8 * k : 8 * k + 8]
+                for w in range(TILES):
+                    at, lanes = g * TILES + w, slice(w * LANES, (w + 1) * LANES)
+                    step_f[at, b * (BLOCK // 8) + k] = step[8 * k : 8 * k + 8, lanes]
+                    grad_f[at, b * (BLOCK // 8) + k] = grad[8 * k : 8 * k + 8, lanes]
                 total = total + step[8 * k : 8 * k + 8]
             return total
 
@@ -120,8 +128,8 @@
                 tile, sub = b * (BLOCK // 8) + i // 8, i % 8
                 out = out_rep[b * BLOCK + i]
                 for w in range(TILES):
-                    step = step_f[tile, sub : sub + 1, columns(g, w)]
-                    grad = grad_f[tile, sub : sub + 1, columns(g, w)]
+                    step = row(step_f, g * TILES + w, tile, sub)
+                    grad = row(grad_f, g * TILES + w, tile, sub)
                     carry[w] = jnp.exp2(step * rate[w]) * (out * grad + carry[w])
             return tuple(carry)
 
@@ -229,11 +237,13 @@
         cols = pl.ds(g * width, width)
 
         def widen(b, _):
-            at = pl.ds(pl.multiple_of(b * BLOCK, BLOCK), BLOCK)
-            part = input_bf[at, cols].astype(jnp.float32)
+            block = pl.ds(pl.multiple_of(b * BLOCK, BLOCK), BLOCK)
+            part = input_bf[block, cols].astype(jnp.float32)
             for k in range(BLOCK // 8):
                 tile = b * (BLOCK // 8) + k
-                x_f[tile, :, cols] = part[8 * k : 8 * k + 8] * step_f[tile, :, cols]
+                for w in range(TILES):
+                    at, lanes = g * TILES + w, slice(w * LANES, (w + 1) * LANES)
+                    x_f[at, tile] = part[8 * k : 8 * k + 8, lanes] * step_f[at, tile]
             return 0
 
         lax.fori_loop(0, blocks, widen, 0)
@@ -259,9 +269,9 @@
                 out, inn = out_rep[at], in_rep[at]
                 products = None
                 for w in range(TILES):
-                    step = step_f[tile, sub : sub + 1, columns(g, w)]
-                    grad = grad_f[tile, sub : sub + 1, columns(g, w)]
-                    x = x_f[tile, sub : sub + 1, columns(g, w)]
+                    step = row(step_f, g * TILES + w, tile, sub)
+                    grad = row(grad_f, g * TILES + w, tile, sub)
+                    x = row(x_f, g * TILES + w, tile, sub)
                     adjoint = out * grad + carry[w]
                     weighted = inn * adjoint
                     folded = weighted[:8]
@@ -286,8 +296,8 @@
                     for s in range(1, 8):
                         total = total + transposer[w, pl.ds(64 * h + s, 8, stride=8), :]
                     results.append(
-                        step_f[tile, :, columns(g, w)] * total
-                        + gain[w] * grad_f[tile, :, columns(g, w)]
+                        step_f[g * TILES + w, tile] * total
+                        + gain[w] * grad_f[g * TILES + w, tile]
                     )
                 dx_bf[pl.ds(pl.multiple_of(b * BLOCK, BLOCK), BLOCK), columns(g, w)] = (
                     jnp.concatenate(results, axis=0).astype(jnp.bfloat16)
@@ -340,6 +350,7 @@
         advance(g, 1)
         for earlier in range(g - 1, -1, -1):
             advance(earlier, g - earlier + 1)
+    repeat(in_ref, in_rep)
     for g in range(groups):
         for later in range(groups - 1, g, -1):
             advance(later, groups + g - later + 1)
@@ -402,9 +413,9 @@
             pltpu.VMEM((rows, channels), bf16),
             pltpu.VMEM((rows, channels), bf16),
             pltpu.VMEM((rows, channels), bf16),
-            pltpu.VMEM((rows // 8, 8, channels), f32),
-            pltpu.VMEM((rows // 8, 8, channels), f32),
-            pltpu.VMEM((rows // 8, 8, channels), f32),
+            pltpu.VMEM((channels // LANES, rows // 8, 8, LANES), f32),
+            pltpu.VMEM((channels // LANES, rows // 8, 8, LANES), f32),
+            pltpu.VMEM((channels // LANES, rows // 8, 8, LANES), f32),
             pltpu.VMEM((rows, states, LANES), f32),
             pltpu.VMEM((rows, states, LANES), f32),
             pltpu.VMEM((rows, states, LANES), f32),
@@ -428,13 +439,13 @@
             pltpu.SemaphoreType.DMA((2, n_exp)),
         ],
         compiler_params=pltpu.CompilerParams(
-            collective_id=0, has_side_effects=True, vmem_limit_bytes=48 * 1024 * 1024
+            collective_id=0, has_side_effects=True, vmem_limit_bytes=64 * 1024 * 1024
         ),
         cost_estimate=pl.CostEstimate(
             flops=14 * work, bytes_accessed=8 * rows * channels, transcendentals=2 * work
         ),
     )(
-        scan_grad, step_size, scan_input, state_in, state_out, decay_rate,
+        scan_grad, step_size, scan_input, state_in.T, state_out.T, decay_rate,
         skip_gain.reshape(1, channels),
     )
 

time: 44 us -> 40.4 us (0.918)
  local copies, waits for them, and re-layouts: 6.8 us -> 2.91 us
  Pallas kernels: 36.2 us -> 36.7 us
    unnamed x16 -> x4, local copies, waits for them, and re-layouts: 6.8 us -> 2.91 us
    pallas_call x1, Pallas kernels: 36.2 us -> 36.7 us  [shards(): pl.pallas_call(functools.partial(kernel, n_ctx, n_exp, 1.0 / math.sqrt(ch...]
where the time goes in v2:
time: 40.4 us; the launch traced here: 40.3 us
  Pallas kernels  36.7 us (91%)
  local copies, waits for them, and re-layouts  2.91 us (7%)
  between operations  0.65 us (2%)
    pallas_call x1, Pallas kernels, shards(): pl.pallas_call(functools.partial(kernel, n_ctx, n_exp, 1.0 / math.sqrt(ch...  36.7 us
    unnamed x4, local copies, waits for them, and re-layouts  2.91 us

profile of v2, /device:TPU:0, one launch (start us, length us, event | category | flops | bytes accessed | tf_op | source)
XLA Modules:
  0.0 40.3 jit_solution(7078521503733265609)
XLA Ops:
  0.6 36.7 %shard_map.86 = (bf16[256,2048]{1,0:T(8,128)(2,1)}, f32[16,64]{1,0:T(8,128)}) custom-call(bf16[256,2048]{1,0:T(8,128)(2,1)} %grad_hbm.1, bf16[256,2048]{1,0:T(8,128)(2,1)} %step_hbm.1, bf16[256,2048]{1,0:T(8,128)(2,1)} %input_hbm.1, f32[16,256]{1,0:T(8,128)} %bitcast.3, f32[16,256]{1,0:T(8,128)} %bitcast.4, f32[16,2048]{1,0:T(8,128)} %rate_ref.1, ...), custom_call_target="tpu_custom_call" | custom-call | flops 117440512 | bytes 4194304 | tf_op jit(solution)/shard_map/pallas_call | solution.py:403
  37.4 0.0 copy-start
  37.4 2.3 %copy.11 = bf16[256,2048]{1,0:T(8,128)(2,1)} copy(bf16[256,2048]{1,0:T(8,128)(2,1)} %get-tuple-element.4) | data formatting | bytes 2097152
  39.7 0.0 copy-done
  39.7 0.6 %copy.12 = f32[16,64]{1,0:T(8,128)} copy(f32[16,64]{1,0:T(8,128)S(1)} %copy-done) | data formatting | bytes 8192
Async XLA Ops:
  37.4 2.3 %copy-start = (f32[16,64]{1,0:T(8,128)S(1)}, f32[16,64]{1,0:T(8,128)}, u32[]{:S(2)}) copy-start(f32[16,64]{1,0:T(8,128)} %get-tuple-element.5) | copy-start | bytes 12292

commit v3 on v2

--- a/solution.py
+++ b/solution.py
@@ -20,7 +20,7 @@
     grad_hbm, step_hbm, input_hbm, in_ref, out_ref, rate_ref, gain_ref,
     dx_hbm, db_ref,
     grad_bf, step_bf, input_bf, dx_bf,
-    grad_f, step_f, x_f, in_rep, out_rep, partial, transposer, rate2,
+    grad_f, step_f, x_f, in_rep, out_rep, partial, rate2,
     summary, got_a, window, got_b, incoming_e, keep, give, got_c,
     share, got_share,
     load_sem, store_sem, a_sem, b_sem, c_sem, r_sem,
@@ -230,6 +230,18 @@
             stage(g, done[g])
             done[g] += 1
 
+    sublane = lax.broadcasted_iota(jnp.int32, (8, LANES), 0)
+
+    def merge(stack, level, value):
+        if level < 3 and stack and stack[-1][0] == level:
+            later = stack.pop()[1]
+            first = (sublane // (1 << level)) % 2 == 0
+            stay = jnp.where(first, value, later)
+            move = jnp.where(first, later, value)
+            merge(stack, level + 1, stay + pltpu.roll(move, 8 - (1 << level), 0))
+        else:
+            stack.append((level, value))
+
     lane_index = lax.broadcasted_iota(jnp.int32, (states, LANES), 1)
 
     def second_sweep(g):
@@ -263,6 +275,7 @@
             carry, sums = list(state[0]), state[1]
             per_section = section // BLOCK
             b = (q + 1) * per_section - 1 - k
+            stacks = [[] for _ in range(TILES)]
             for i in range(BLOCK - 1, -1, -1):
                 tile, sub = b * (BLOCK // 8) + i // 8, i % 8
                 at = b * BLOCK + i
@@ -277,7 +290,7 @@
                     folded = weighted[:8]
                     for s in range(8, states, 8):
                         folded = folded + weighted[s : s + 8]
-                    transposer[w, 8 * i : 8 * i + 8, :] = folded
+                    merge(stacks[w], 0, folded)
                     product = adjoint * x
                     products = product if products is None else products + product
                     carry[w] = jnp.exp2(step * rate[w]) * adjoint
@@ -292,9 +305,7 @@
                 results = []
                 for h in range(BLOCK // 8):
                     tile = b * (BLOCK // 8) + h
-                    total = transposer[w, pl.ds(64 * h, 8, stride=8), :]
-                    for s in range(1, 8):
-                        total = total + transposer[w, pl.ds(64 * h + s, 8, stride=8), :]
+                    total = stacks[w][BLOCK // 8 - 1 - h][1]
                     results.append(
                         step_f[g * TILES + w, tile] * total
                         + gain[w] * grad_f[g * TILES + w, tile]
@@ -397,6 +408,7 @@
     groups, half = channels // width, width // 2
     hops = max(1, (n_ctx // 2 - 1).bit_length())
     f32, bf16 = jnp.float32, jnp.bfloat16
+    hbm = pl.BlockSpec(memory_space=pltpu.HBM)
     any_spec = pl.BlockSpec(memory_space=pl.ANY)
     vmem = pl.BlockSpec(memory_space=pltpu.VMEM)
     work = rows * channels * states
@@ -406,7 +418,7 @@
             jax.ShapeDtypeStruct((rows, channels), bf16),
             jax.ShapeDtypeStruct((states, rows // n_exp), f32),
         ),
-        in_specs=[any_spec, any_spec, any_spec, vmem, vmem, vmem, vmem],
+        in_specs=[hbm, hbm, hbm, vmem, vmem, vmem, vmem],
         out_specs=(any_spec, vmem),
         scratch_shapes=[
             pltpu.VMEM((rows, channels), bf16),
@@ -419,7 +431,6 @@
             pltpu.VMEM((rows, states, LANES), f32),
             pltpu.VMEM((rows, states, LANES), f32),
             pltpu.VMEM((rows, states, LANES), f32),
-            pltpu.VMEM((TILES, 8 * BLOCK, LANES), f32),
             pltpu.VMEM((groups, 2, states, half), f32),
             pltpu.VMEM((groups, 2, states + 8, half), f32),
             pltpu.VMEM((groups, states + 8, half), f32),
@@ -439,7 +450,7 @@
             pltpu.SemaphoreType.DMA((2, n_exp)),
         ],
         compiler_params=pltpu.CompilerParams(
-            collective_id=0, has_side_effects=True, vmem_limit_bytes=64 * 1024 * 1024
+            collective_id=0, has_side_effects=True, vmem_limit_bytes=62 * 1024 * 1024
         ),
         cost_estimate=pl.CostEstimate(
             flops=14 * work, bytes_accessed=8 * rows * channels, transcendentals=2 * work

time: 40.4 us -> 40.8 us (level)
  no operation moved by 1% of the time
where the time goes in v3:
time: 40.8 us; the launch traced here: 40.6 us
  Pallas kernels  37.1 us (91%)
  local copies, waits for them, and re-layouts  2.91 us (7%)
  between operations  0.65 us (2%)
    pallas_call x1, Pallas kernels, shards(): pl.pallas_call(functools.partial(kernel, n_ctx, n_exp, 1.0 / math.sqrt(ch...  37.1 us
    unnamed x4, local copies, waits for them, and re-layouts  2.91 us

profile of v3, /device:TPU:0, one launch (start us, length us, event | category | flops | bytes accessed | tf_op | source)
XLA Modules:
  0.0 40.6 jit_solution(15241774096503972161)
XLA Ops:
  0.6 37.1 %shard_map.86 = (bf16[256,2048]{1,0:T(8,128)(2,1)}, f32[16,64]{1,0:T(8,128)}) custom-call(bf16[256,2048]{1,0:T(8,128)(2,1)} %grad_hbm.1, bf16[256,2048]{1,0:T(8,128)(2,1)} %step_hbm.1, bf16[256,2048]{1,0:T(8,128)(2,1)} %input_hbm.1, f32[16,256]{1,0:T(8,128)} %bitcast.3, f32[16,256]{1,0:T(8,128)} %bitcast.4, f32[16,2048]{1,0:T(8,128)} %rate_ref.1, ...), custom_call_target="tpu_custom_call" | custom-call | flops 117440512 | bytes 4194304 | tf_op jit(solution)/shard_map/pallas_call | solution.py:415
  37.7 0.0 copy-start
  37.7 2.3 %copy.11 = bf16[256,2048]{1,0:T(8,128)(2,1)} copy(bf16[256,2048]{1,0:T(8,128)(2,1)} %get-tuple-element.4) | data formatting | bytes 2097152
  40.0 0.0 copy-done
  40.0 0.6 %copy.12 = f32[16,64]{1,0:T(8,128)} copy(f32[16,64]{1,0:T(8,128)S(1)} %copy-done) | data formatting | bytes 8192
Async XLA Ops:
  37.7 2.3 %copy-start = (f32[16,64]{1,0:T(8,128)S(1)}, f32[16,64]{1,0:T(8,128)}, u32[]{:S(2)}) copy-start(f32[16,64]{1,0:T(8,128)} %get-tuple-element.5) | copy-start | bytes 12292

commit v4 on v2

--- a/solution.py
+++ b/solution.py
@@ -20,7 +20,7 @@
     grad_hbm, step_hbm, input_hbm, in_ref, out_ref, rate_ref, gain_ref,
     dx_hbm, db_ref,
     grad_bf, step_bf, input_bf, dx_bf,
-    grad_f, step_f, x_f, in_rep, out_rep, partial, transposer, rate2,
+    grad_f, step_f, x_f, in_rep, out_rep, partial, transposer, decays, rate2,
     summary, got_a, window, got_b, incoming_e, keep, give, got_c,
     share, got_share,
     load_sem, store_sem, a_sem, b_sem, c_sem, r_sem,
@@ -130,7 +130,9 @@
                 for w in range(TILES):
                     step = row(step_f, g * TILES + w, tile, sub)
                     grad = row(grad_f, g * TILES + w, tile, sub)
-                    carry[w] = jnp.exp2(step * rate[w]) * (out * grad + carry[w])
+                    factor = jnp.exp2(step * rate[w])
+                    decays[g, b * BLOCK + i, :, w * LANES : (w + 1) * LANES] = factor
+                    carry[w] = factor * (out * grad + carry[w])
             return tuple(carry)
 
         zero = jnp.zeros((states, LANES), jnp.float32)
@@ -247,7 +249,6 @@
             return 0
 
         lax.fori_loop(0, blocks, widen, 0)
-        rate = rates(g)
         copy_c(g).wait_recv()
         mine, other = keep[g], got_c[g]
         halves = (jnp.where(low, mine, other), jnp.where(low, other, mine))
@@ -269,7 +270,6 @@
                 out, inn = out_rep[at], in_rep[at]
                 products = None
                 for w in range(TILES):
-                    step = row(step_f, g * TILES + w, tile, sub)
                     grad = row(grad_f, g * TILES + w, tile, sub)
                     x = row(x_f, g * TILES + w, tile, sub)
                     adjoint = out * grad + carry[w]
@@ -280,7 +280,7 @@
                     transposer[w, 8 * i : 8 * i + 8, :] = folded
                     product = adjoint * x
                     products = product if products is None else products + product
-                    carry[w] = jnp.exp2(step * rate[w]) * adjoint
+                    carry[w] = decays[g, at, :, w * LANES : (w + 1) * LANES] * adjoint
                 if g > 0:
                     products = products + partial[at]
                 if last:
@@ -420,6 +420,7 @@
             pltpu.VMEM((rows, states, LANES), f32),
             pltpu.VMEM((rows, states, LANES), f32),
             pltpu.VMEM((TILES, 8 * BLOCK, LANES), f32),
+            pltpu.VMEM((groups, rows, states, width), f32),
             pltpu.VMEM((groups, 2, states, half), f32),
             pltpu.VMEM((groups, 2, states + 8, half), f32),
             pltpu.VMEM((groups, states + 8, half), f32),
@@ -439,7 +440,7 @@
             pltpu.SemaphoreType.DMA((2, n_exp)),
         ],
         compiler_params=pltpu.CompilerParams(
-            collective_id=0, has_side_effects=True, vmem_limit_bytes=64 * 1024 * 1024
+            collective_id=0, has_side_effects=True, vmem_limit_bytes=62 * 1024 * 1024
         ),
         cost_estimate=pl.CostEstimate(
             flops=14 * work, bytes_accessed=8 * rows * channels, transcendentals=2 * work

time: 40.4 us -> 38.9 us (0.963)
  Pallas kernels: 36.7 us -> 35.2 us
    pallas_call x1, Pallas kernels: 36.7 us -> 35.2 us  [shards(): pl.pallas_call(functools.partial(kernel, n_ctx, n_exp, 1.0 / math.sqrt(ch...]
where the time goes in v4:
time: 38.9 us; the launch traced here: 38.7 us
  Pallas kernels  35.2 us (90%)
  local copies, waits for them, and re-layouts  2.91 us (7%)
  between operations  0.65 us (2%)
    pallas_call x1, Pallas kernels, shards(): pl.pallas_call(functools.partial(kernel, n_ctx, n_exp, 1.0 / math.sqrt(ch...  35.2 us
    unnamed x4, local copies, waits for them, and re-layouts  2.91 us

profile of v4, /device:TPU:0, one launch (start us, length us, event | category | flops | bytes accessed | tf_op | source)
XLA Modules:
  0.0 38.7 jit_solution(1122825714015406502)
XLA Ops:
  0.6 35.2 %shard_map.86 = (bf16[256,2048]{1,0:T(8,128)(2,1)}, f32[16,64]{1,0:T(8,128)}) custom-call(bf16[256,2048]{1,0:T(8,128)(2,1)} %grad_hbm.1, bf16[256,2048]{1,0:T(8,128)(2,1)} %step_hbm.1, bf16[256,2048]{1,0:T(8,128)(2,1)} %input_hbm.1, f32[16,256]{1,0:T(8,128)} %bitcast.3, f32[16,256]{1,0:T(8,128)} %bitcast.4, f32[16,2048]{1,0:T(8,128)} %rate_ref.1, ...), custom_call_target="tpu_custom_call" | custom-call | flops 117440512 | bytes 4194304 | tf_op jit(solution)/shard_map/pallas_call | solution.py:403
  35.8 0.0 copy-start
  35.8 2.3 %copy.11 = bf16[256,2048]{1,0:T(8,128)(2,1)} copy(bf16[256,2048]{1,0:T(8,128)(2,1)} %get-tuple-element.4) | data formatting | bytes 2097152
  38.1 0.0 copy-done
  38.1 0.6 %copy.12 = f32[16,64]{1,0:T(8,128)} copy(f32[16,64]{1,0:T(8,128)S(1)} %copy-done) | data formatting | bytes 8192
Async XLA Ops:
  35.8 2.3 %copy-start = (f32[16,64]{1,0:T(8,128)S(1)}, f32[16,64]{1,0:T(8,128)}, u32[]{:S(2)}) copy-start(f32[16,64]{1,0:T(8,128)} %get-tuple-element.5) | copy-start | bytes 12292

commit v5 on v4

--- a/solution.py
+++ b/solution.py
@@ -12,7 +12,16 @@
 LANES = 128
 TILES = 4
 BLOCK = 16
+FAN = 4
 LOG2E = math.log2(math.e)
+
+
+def steps_over(pairs):
+    hops, hop = [], 1
+    while hop < pairs:
+        hops.append(hop)
+        hop *= FAN
+    return hops
 
 
 def kernel(
@@ -33,9 +42,8 @@
     blocks = rows // BLOCK
     section = rows // n_exp
     pairs = n_ctx // 2
-    hops = []
-    while (1 << len(hops)) < pairs:
-        hops.append(1 << len(hops))
+    hops = steps_over(pairs)
+    distances = [j * hop for hop in hops for j in range(1, FAN)]
 
     ctx, me = lax.axis_index("ctx"), lax.axis_index("exp")
     side = lax.rem(ctx, 2)
@@ -61,7 +69,7 @@
         pl.semaphore_signal(
             barrier, inc=1, device_id=(ctx, lax.rem(me + other, n_exp)), device_id_type=MESH
         )
-    for hop in hops:
+    for hop in distances:
 
         @pl.when(pair + hop < pairs)
         def _():
@@ -152,11 +160,12 @@
             device_id=(partner, me), device_id_type=MESH,
         )
 
-    def copy_b(g, k):
+    def copy_b(g, k, j):
+        slot = k * (FAN - 1) + j - 1
         return pltpu.make_async_remote_copy(
-            src_ref=window.at[g, k], dst_ref=got_b.at[g, k],
-            send_sem=b_sem.at[0, g, k], recv_sem=b_sem.at[1, g, k],
-            device_id=(ctx - 2 * hops[k], me), device_id_type=MESH,
+            src_ref=window.at[g, k], dst_ref=got_b.at[g, slot],
+            send_sem=b_sem.at[0, g, slot], recv_sem=b_sem.at[1, g, slot],
+            device_id=(ctx - 2 * j * hops[k], me), device_id_type=MESH,
         )
 
     def copy_c(g):
@@ -174,9 +183,11 @@
         return jnp.exp2(rate * jnp.concatenate([reach] * (states // 8), axis=0))
 
     def send_b(g, k):
-        @pl.when(pair >= hops[k])
-        def _():
-            copy_b(g, k).start()
+        for j in range(1, FAN):
+
+            @pl.when(pair >= j * hops[k])
+            def _():
+                copy_b(g, k, j).start()
 
     def finish(g):
         first, second = both_sides(g)
@@ -205,14 +216,16 @@
         k = s - 2
         rate = rate2[g, side]
 
-        @pl.when(pair + hops[k] < pairs)
-        def _():
-            copy_b(g, k).wait_recv()
-            entering, got = incoming_e[g], got_b[g, k]
-            incoming_e[g, :states] = (
-                entering[:states] + decay(rate, entering[states:]) * got[:states]
-            )
-            incoming_e[g, states:] = entering[states:] + got[states:]
+        for j in range(1, FAN):
+
+            @pl.when(pair + j * hops[k] < pairs)
+            def _():
+                copy_b(g, k, j).wait_recv()
+                entering, got = incoming_e[g], got_b[g, k * (FAN - 1) + j - 1]
+                incoming_e[g, :states] = (
+                    entering[:states] + decay(rate, entering[states:]) * got[:states]
+                )
+                incoming_e[g, states:] = entering[states:] + got[states:]
 
         if k + 1 < len(hops):
             mine, entering = window[g, 0], incoming_e[g]
@@ -234,7 +247,7 @@
 
     lane_index = lax.broadcasted_iota(jnp.int32, (states, LANES), 1)
 
-    def second_sweep(g):
+    def weigh_inputs(g):
         load(2, g).wait()
         cols = pl.ds(g * width, width)
 
@@ -249,6 +262,8 @@
             return 0
 
         lax.fori_loop(0, blocks, widen, 0)
+
+    def second_sweep(g):
         copy_c(g).wait_recv()
         mine, other = keep[g], got_c[g]
         halves = (jnp.where(low, mine, other), jnp.where(low, other, mine))
@@ -348,13 +363,18 @@
         if g == 0:
             pl.semaphore_wait(barrier, count)
         advance(g, 1)
-        for earlier in range(g - 1, -1, -1):
-            advance(earlier, g - earlier + 1)
+        if g >= 2:
+            advance(g - 2, 2)
     repeat(in_ref, in_rep)
-    for g in range(groups):
-        for later in range(groups - 1, g, -1):
-            advance(later, groups + g - later + 1)
-        advance(g, stages)
+    advance(0, 3)
+    for g in range(groups):
+        weigh_inputs(g)
+    for g in range(1, groups):
+        advance(g, 2)
+    advance(min(1, groups - 1), 3)
+    for g in range(groups):
+        for later in range(g, groups if g > 0 else 1):
+            advance(later, stages)
         second_sweep(g)
 
     total = share[me]
@@ -383,10 +403,11 @@
         copy_a(g).wait_send()
         copy_c(g).wait_send()
         for k, hop in enumerate(hops):
-
-            @pl.when(pair >= hop)
-            def _():
-                copy_b(g, k).wait_send()
+            for j in range(1, FAN):
+
+                @pl.when(pair >= j * hop)
+                def _():
+                    copy_b(g, k, j).wait_send()
 
 
 def shards(scan_grad, step_size, scan_input, state_in, state_out, decay_rate, skip_gain):
@@ -395,7 +416,8 @@
     states = state_in.shape[1]
     width = TILES * LANES
     groups, half = channels // width, width // 2
-    hops = max(1, (n_ctx // 2 - 1).bit_length())
+    hops = max(1, len(steps_over(n_ctx // 2)))
+    slots = hops * (FAN - 1)
     f32, bf16 = jnp.float32, jnp.bfloat16
     any_spec = pl.BlockSpec(memory_space=pl.ANY)
     vmem = pl.BlockSpec(memory_space=pltpu.VMEM)
@@ -425,7 +447,7 @@
             pltpu.VMEM((groups, 2, states + 8, half), f32),
             pltpu.VMEM((groups, states + 8, half), f32),
             pltpu.VMEM((groups, hops, states + 8, half), f32),
-            pltpu.VMEM((groups, hops, states + 8, half), f32),
+            pltpu.VMEM((groups, slots, states + 8, half), f32),
             pltpu.VMEM((groups, states + 8, half), f32),
             pltpu.VMEM((groups, states, half), f32),
             pltpu.VMEM((groups, states, half), f32),
@@ -435,7 +457,7 @@
             pltpu.SemaphoreType.DMA((3, groups)),
             pltpu.SemaphoreType.DMA((groups,)),
             pltpu.SemaphoreType.DMA((2, groups)),
-            pltpu.SemaphoreType.DMA((2, groups, hops)),
+            pltpu.SemaphoreType.DMA((2, groups, slots)),
             pltpu.SemaphoreType.DMA((2, groups)),
             pltpu.SemaphoreType.DMA((2, n_exp)),
         ],

time: 38.9 us -> 37.3 us (0.959)
  Pallas kernels: 35.2 us -> 33.6 us
    pallas_call x1, Pallas kernels: 35.2 us -> 33.6 us  [shards(): pl.pallas_call(functools.partial(kernel, n_ctx, n_exp, 1.0 / math.sqrt(ch...]
where the time goes in v5:
time: 37.3 us; the launch traced here: 37.1 us
  Pallas kernels  33.6 us (90%)
  local copies, waits for them, and re-layouts  2.91 us (8%)
  between operations  0.65 us (2%)
    pallas_call x1, Pallas kernels, shards(): pl.pallas_call(functools.partial(kernel, n_ctx, n_exp, 1.0 / math.sqrt(ch...  33.6 us
    unnamed x4, local copies, waits for them, and re-layouts  2.91 us

profile of v5, /device:TPU:0, one launch (start us, length us, event | category | flops | bytes accessed | tf_op | source)
XLA Modules:
  0.0 37.1 jit_solution(6648446100177621146)
XLA Ops:
  0.6 33.6 %shard_map.86 = (bf16[256,2048]{1,0:T(8,128)(2,1)}, f32[16,64]{1,0:T(8,128)}) custom-call(bf16[256,2048]{1,0:T(8,128)(2,1)} %grad_hbm.1, bf16[256,2048]{1,0:T(8,128)(2,1)} %step_hbm.1, bf16[256,2048]{1,0:T(8,128)(2,1)} %input_hbm.1, f32[16,256]{1,0:T(8,128)} %bitcast.3, f32[16,256]{1,0:T(8,128)} %bitcast.4, f32[16,2048]{1,0:T(8,128)} %rate_ref.1, ...), custom_call_target="tpu_custom_call" | custom-call | flops 117440512 | bytes 4194304 | tf_op jit(solution)/shard_map/pallas_call | solution.py:425
  34.2 0.0 copy-start
  34.2 2.3 %copy.11 = bf16[256,2048]{1,0:T(8,128)(2,1)} copy(bf16[256,2048]{1,0:T(8,128)(2,1)} %get-tuple-element.4) | data formatting | bytes 2097152
  36.5 0.0 copy-done
  36.5 0.6 %copy.12 = f32[16,64]{1,0:T(8,128)} copy(f32[16,64]{1,0:T(8,128)S(1)} %copy-done) | data formatting | bytes 8192
Async XLA Ops:
  34.2 2.3 %copy-start = (f32[16,64]{1,0:T(8,128)S(1)}, f32[16,64]{1,0:T(8,128)}, u32[]{:S(2)}) copy-start(f32[16,64]{1,0:T(8,128)} %get-tuple-element.5) | copy-start | bytes 12292

commit v6 on v5

--- a/solution.py
+++ b/solution.py
@@ -11,7 +11,8 @@
 MESH = pl.DeviceIdType.MESH
 LANES = 128
 TILES = 4
-BLOCK = 16
+BLOCK = 32
+WIDE = 128
 FAN = 4
 LOG2E = math.log2(math.e)
 
@@ -115,18 +116,18 @@
         cols = pl.ds(g * width, width)
 
         def widen(b, total):
-            block = pl.ds(pl.multiple_of(b * BLOCK, BLOCK), BLOCK)
+            block = pl.ds(pl.multiple_of(b * WIDE, WIDE), WIDE)
             step = step_bf[block, cols].astype(jnp.float32)
             grad = grad_bf[block, cols].astype(jnp.float32)
-            for k in range(BLOCK // 8):
+            for k in range(WIDE // 8):
                 for w in range(TILES):
                     at, lanes = g * TILES + w, slice(w * LANES, (w + 1) * LANES)
-                    step_f[at, b * (BLOCK // 8) + k] = step[8 * k : 8 * k + 8, lanes]
-                    grad_f[at, b * (BLOCK // 8) + k] = grad[8 * k : 8 * k + 8, lanes]
+                    step_f[at, b * (WIDE // 8) + k] = step[8 * k : 8 * k + 8, lanes]
+                    grad_f[at, b * (WIDE // 8) + k] = grad[8 * k : 8 * k + 8, lanes]
                 total = total + step[8 * k : 8 * k + 8]
             return total
 
-        total = lax.fori_loop(0, blocks, widen, jnp.zeros((8, width), jnp.float32))
+        total = lax.fori_loop(0, rows // WIDE, widen, jnp.zeros((8, width), jnp.float32))
         rate = rates(g)
 
         def sweep(k, carry):
@@ -252,16 +253,16 @@
         cols = pl.ds(g * width, width)
 
         def widen(b, _):
-            block = pl.ds(pl.multiple_of(b * BLOCK, BLOCK), BLOCK)
+            block = pl.ds(pl.multiple_of(b * WIDE, WIDE), WIDE)
             part = input_bf[block, cols].astype(jnp.float32)
-            for k in range(BLOCK // 8):
-                tile = b * (BLOCK // 8) + k
+            for k in range(WIDE // 8):
+                tile = b * (WIDE // 8) + k
                 for w in range(TILES):
                     at, lanes = g * TILES + w, slice(w * LANES, (w + 1) * LANES)
                     x_f[at, tile] = part[8 * k : 8 * k + 8, lanes] * step_f[at, tile]
             return 0
 
-        lax.fori_loop(0, blocks, widen, 0)
+        lax.fori_loop(0, rows // WIDE, widen, 0)
 
     def second_sweep(g):
         copy_c(g).wait_recv()

time: 37.3 us -> 36.2 us (0.971)
  Pallas kernels: 33.6 us -> 32.5 us
    pallas_call x1, Pallas kernels: 33.6 us -> 32.5 us  [shards(): pl.pallas_call(functools.partial(kernel, n_ctx, n_exp, 1.0 / math.sqrt(ch...]
where the time goes in v6:
time: 36.2 us; the launch traced here: 36 us
  Pallas kernels  32.5 us (90%)
  local copies, waits for them, and re-layouts  2.91 us (8%)
  between operations  0.65 us (2%)
    pallas_call x1, Pallas kernels, shards(): pl.pallas_call(functools.partial(kernel, n_ctx, n_exp, 1.0 / math.sqrt(ch...  32.5 us
    unnamed x4, local copies, waits for them, and re-layouts  2.91 us

profile of v6, /device:TPU:0, one launch (start us, length us, event | category | flops | bytes accessed | tf_op | source)
XLA Modules:
  0.0 36.0 jit_solution(4431552636396366564)
XLA Ops:
  0.6 32.5 %shard_map.86 = (bf16[256,2048]{1,0:T(8,128)(2,1)}, f32[16,64]{1,0:T(8,128)}) custom-call(bf16[256,2048]{1,0:T(8,128)(2,1)} %grad_hbm.1, bf16[256,2048]{1,0:T(8,128)(2,1)} %step_hbm.1, bf16[256,2048]{1,0:T(8,128)(2,1)} %input_hbm.1, f32[16,256]{1,0:T(8,128)} %bitcast.3, f32[16,256]{1,0:T(8,128)} %bitcast.4, f32[16,2048]{1,0:T(8,128)} %rate_ref.1, ...), custom_call_target="tpu_custom_call" | custom-call | flops 117440512 | bytes 4194304 | tf_op jit(solution)/shard_map/pallas_call | solution.py:426
  33.1 0.0 copy-start
  33.1 2.3 %copy.11 = bf16[256,2048]{1,0:T(8,128)(2,1)} copy(bf16[256,2048]{1,0:T(8,128)(2,1)} %get-tuple-element.4) | data formatting | bytes 2097152
  35.4 0.0 copy-done
  35.4 0.6 %copy.12 = f32[16,64]{1,0:T(8,128)} copy(f32[16,64]{1,0:T(8,128)S(1)} %copy-done) | data formatting | bytes 8192
Async XLA Ops:
  33.1 2.3 %copy-start = (f32[16,64]{1,0:T(8,128)S(1)}, f32[16,64]{1,0:T(8,128)}, u32[]{:S(2)}) copy-start(f32[16,64]{1,0:T(8,128)} %get-tuple-element.5) | copy-start | bytes 12292
